TPU v7x, 128 devices: a whole 4x4x4 slice. The times are simulated.
128 devices in a mesh: gx: 8 (over x, z_lo), gy: 16 (over z_hi, y, core).
Axes of the slice: x: 4, y: 4, z: 4 (z_hi: 2, z_lo: 2; z = z_hi * 2 + z_lo), core: 2. Of those that a mesh axis runs over, the one named last changes fastest.
Arguments:
- displacement: float32 [2, 3, 8, 1024, 2048], P(None, None, None, 'gx', 'gy'), may hold values from -0.6 to 0.6
- velocity: float32 [2, 3, 8, 1024, 2048], P(None, None, None, 'gx', 'gy'), may hold values from -3 to 3
- modulus: float32 [2, 8, 1024, 2048], P(None, None, 'gx', 'gy'), may hold values from 0.5 to 2
- density: float32 [2, 8, 1024, 2048], P(None, None, 'gx', 'gy'), may hold values from 1 to 4
- clearance: float32 [1024, 2048], P('gx', 'gy'), may hold values from -0.3 to 0.3
- mortar_coupling: float32 [128, 128], replicated, may hold values from -0.5 to 0.5
- pair_owner: int32 [8, 4096, 1], P('gx', 'gy'), may hold values from 0 to 15; in each aligned block of 256 rows (0 to 255, 256 to 511, ..., all dimensions but the last counted through in order) at most 64 rows name the same one
- pair_row: int32 [8, 4096, 1], P('gx', 'gy'), may hold values from 0 to 127
- pair_offset: int32 [8, 4096, 1], P('gx', 'gy'), may hold values from 0 to 127
- pair_active: int32 [8, 4096, 1], P('gx', 'gy'), may hold values 0 or 1
Outputs:
- new_displacement: float32 [2, 3, 8, 1024, 2048], P(None, None, None, 'gx', 'gy')
- new_velocity: float32 [2, 3, 8, 1024, 2048], P(None, None, None, 'gx', 'gy')
Inputs may be any that keep to these rules, and one draw needn't show every extreme that they name: `pair_owner`: in the pairs of one device, at most 64 name one owner, and one owner is named by exactly 64 pairs of some device.
All inputs are finite; a program needn't handle non-finite values. No bound on the sum of `pair_active` on one device may be relied on, other than what follows from the above.
Results may differ from a plain program's by a relative error of at most 0.0001.
Values sent between devices are 32-bit elements; how exact they have to be, the bound alone decides.
A program may use at most 192 MiB of HBM per device.

v0:
```python
import functools

import jax
import jax.numpy as jnp
from jax import lax
from jax.experimental import pallas as pl
from jax.experimental.pallas import tpu as pltpu
from jax.sharding import PartitionSpec as P

STEPS = 2
LAYERS = 8
TILE = 128
BLOCKS = TILE // 8
PAIRS = 256
GROUPS = 6
MASTER, SLAVE = 2, 5
LOW, MAIN, HIGH = 7, 8, 136

time_step = 0.2
penalty_stiffness = 4.0

MESH = pl.DeviceIdType.MESH
f32 = jnp.float32


def lanes(shape):
    return lax.broadcasted_iota(jnp.int32, shape, len(shape) - 1)


def cyclic_shift(values, offsets, direction):
    for bit in range(7):
        amount = 1 << bit
        rolled = pltpu.roll(values, (direction * amount) % TILE, axis=1)
        values = jnp.where((offsets & amount) != 0, rolled, values)
    return values


def kernel(
    n_gx, n_gy,
    disp, vel, mod, dens, clear, mortar, flat_s, pair_v,
    u_out, v_out,
    U, V, D, L, C, FACES, T, RP, RR, OH, XS, YS, HX, HY, HD, OFFS, ACT, SL, SF, ROWS, DINV,
    load_sem, own_sem, halo_send, halo_recv, face_send, face_recv, pass_send, pass_recv,
    core_send, core_recv, sum_send, sum_recv, store_sem,
):
    gx = lax.axis_index("gx")
    gy = lax.axis_index("gy")
    core = lax.rem(gy, 2)
    chip = gy // 2
    chips = n_gy // 2
    partner = gy + 1 - 2 * core
    up = lax.rem(gx + n_gx - 1, n_gx)
    down = lax.rem(gx + 1, n_gx)
    left = lax.rem(gy + n_gy - 1, n_gy)
    right = lax.rem(gy + 1, n_gy)
    other = lax.rem(gy + n_gy - 1 + 2 * core, n_gy)

    def at(x, y):
        return {"gx": x, "gy": y}

    def mate(q):
        return 2 * lax.rem(chip + q, chips) + core

    loads = [
        pltpu.make_async_copy(disp, U.at[pl.ds(0, GROUPS)], load_sem.at[0]),
        pltpu.make_async_copy(mod, U.at[pl.ds(GROUPS, 2)], load_sem.at[1]),
        pltpu.make_async_copy(dens, D, load_sem.at[2]),
        pltpu.make_async_copy(vel, V, load_sem.at[3]),
    ]
    for load in loads:
        load.start()

    barrier = pltpu.get_barrier_semaphore()
    friends = [at(gx, mate(q)) for q in range(1, chips)]
    friends += [at(gx, partner), at(gx, other)]
    friends += [at(x, y) for x in (up, down) for y in (left, gy, right)]
    for friend in friends:
        pl.semaphore_signal(barrier, inc=1, device_id=friend, device_id_type=MESH)
    pl.semaphore_wait(barrier, len(friends))

    def remote(src, dst, send, recv, target):
        return pltpu.make_async_remote_copy(
            src_ref=src, dst_ref=dst, send_sem=send, recv_sem=recv,
            device_id=target, device_id_type=MESH,
        )

    def block_of(j):
        return pl.ds(pl.multiple_of(j * TILE, TILE), TILE)

    def face_copies(step, src):
        mine = FACES.at[step, block_of(gy)]
        out = [remote(src, mine, face_send.at[step, 0], face_recv.at[step, 0], at(gx, partner))]
        for q in range(1, chips):
            out.append(remote(src, mine, face_send.at[step, q], face_recv.at[step, q], at(gx, mate(q))))
        return out

    def pass_copy(step, q):
        held = FACES.at[step, block_of(mate(chips - q))]
        return remote(held, held, pass_send.at[step, q], pass_recv.at[step, q], at(gx, partner))

    def send_faces(step, src):
        copies = face_copies(step, src)
        for q in [1, chips - 1] + list(range(2, chips - 1)) + [0]:
            copies[q].start()
        own = pltpu.make_async_copy(src, FACES.at[step, block_of(gy)], own_sem.at[step])
        own.start()
        return copies, own

    def finish_faces(step, copies, own):
        passed = []
        for q in [1, chips - 1] + list(range(2, chips - 1)):
            copies[q].wait_recv()
            copy = pass_copy(step, q)
            copy.start()
            passed.append(copy)
        own.wait()
        copies[0].wait_recv()
        for copy in passed:
            copy.wait_recv()
        for copy in copies + passed:
            copy.wait_send()

    def pack(groups):
        def one(g, carry):
            lane = lanes((8, TILE))

            def layer(l, both):
                low, high = both
                for t in range(BLOCKS):
                    spot = l * BLOCKS + t
                    r = pltpu.roll(U[g, l, t * 8 : t * 8 + 8, :], lax.rem(spot + 1, TILE), axis=1)
                    high = jnp.where(lane == spot, r, high)
                    low = jnp.where(lane == lax.rem(spot + 1, TILE), r, low)
                row = g * 8 + l
                XS[0, pl.ds(row, 1), :] = U[g, l, 0:1, :]
                XS[1, pl.ds(row, 1), :] = U[g, l, TILE - 1 : TILE, :]
                return low, high

            zero = jnp.zeros((8, TILE), f32)
            low, high = lax.fori_loop(0, LAYERS, layer, (zero, zero))
            rows = pl.ds(pl.multiple_of(g * 8, 8), 8)
            YS[0, rows, :] = low
            YS[1, rows, :] = high
            return carry

        lax.fori_loop(0, groups, one, 0)

    def halo_copies(step, groups):
        rows = pl.ds(0, groups * 8)
        plan = [
            (XS.at[0, rows], HX.at[step, 1, rows], at(up, gy)),
            (XS.at[1, rows], HX.at[step, 0, rows], at(down, gy)),
            (YS.at[0, rows], HY.at[step, 1, rows], at(gx, left)),
            (YS.at[1, rows], HY.at[step, 0, rows], at(gx, right)),
            (XS.at[0, rows], HD.at[step, 3, rows], at(up, left)),
            (XS.at[0, rows], HD.at[step, 2, rows], at(up, right)),
            (XS.at[1, rows], HD.at[step, 1, rows], at(down, left)),
            (XS.at[1, rows], HD.at[step, 0, rows], at(down, right)),
        ]
        return [
            remote(src, dst, halo_send.at[step, k], halo_recv.at[step, k], target)
            for k, (src, dst, target) in enumerate(plan)
        ]

    def spread(step, first, groups):
        at_top = (gx == 0).astype(f32)
        at_bottom = (gx == n_gx - 1).astype(f32)
        at_left = (gy == 0).astype(f32)
        at_right = (gy == n_gy - 1).astype(f32)

        def one(g, carry):
            is_mod = (g >= GROUPS).astype(f32)
            keep_top, keep_bottom = 1.0 - is_mod * at_top, 1.0 - is_mod * at_bottom
            keep_left, keep_right = 1.0 - is_mod * at_left, 1.0 - is_mod * at_right
            lane = lanes((8, TILE))
            rows = pl.ds(pl.multiple_of(g * 8, 8), 8)
            low = HY[step, 0, rows, :] * keep_left
            high = HY[step, 1, rows, :] * keep_right

            def layer(l, carry):
                for t in range(BLOCKS):
                    turn = TILE - 1 - (l * BLOCKS + t)
                    here = U[g, l, t * 8 : t * 8 + 8, :]
                    after = jnp.where(lane == 0, pltpu.roll(high, turn, axis=1), here)
                    before = jnp.where(lane == TILE - 1, pltpu.roll(low, turn, axis=1), here)
                    into = slice(MAIN + t * 8, MAIN + t * 8 + 8)
                    L[0, g, l, into, :] = pltpu.roll(before, 1, axis=1)
                    L[1, g, l, into, :] = here
                    L[2, g, l, into, :] = pltpu.roll(after, TILE - 1, axis=1)
                return carry

            lax.fori_loop(0, LAYERS, layer, 0)
            for side, keep, spot in ((0, keep_top, LOW), (1, keep_bottom, HIGH)):
                here = HX[step, side, rows, :] * keep
                corner_low = HD[step, 2 * side, rows, :] * (keep * keep_left)
                corner_high = HD[step, 2 * side + 1, rows, :] * (keep * keep_right)
                before = pltpu.roll(jnp.where(lane == TILE - 1, corner_low, here), 1, axis=1)
                after = pltpu.roll(jnp.where(lane == 0, corner_high, here), TILE - 1, axis=1)
                for dy, plane in enumerate((before, here, after)):
                    for l in range(LAYERS):
                        L[dy, g, l, spot : spot + 1, :] = plane[l : l + 1, :]
            return carry

        lax.fori_loop(first, first + groups, one, 0)

    def couplings():
        def one(it, carry):
            b = it // (BLOCKS * LAYERS)
            t = lax.rem(it // LAYERS, BLOCKS)
            l = lax.rem(it, LAYERS)
            row = pl.multiple_of(t * 8, 8)
            own = L[1, GROUPS + b, l, pl.ds(row + MAIN, 8), :]
            base = own * (time_step / D[b, l, pl.ds(row, 8), :])
            total = jnp.zeros((8, TILE), f32)
            for dl in (-1, 0, 1):
                near = jnp.clip(l + dl, 0, LAYERS - 1)
                inside = jnp.logical_and(l + dl >= 0, l + dl < LAYERS).astype(f32)
                scaled = base if dl == 0 else base * inside
                for dx in (-1, 0, 1):
                    for dy in (-1, 0, 1):
                        nonzero = abs(dl) + abs(dx) + abs(dy)
                        if nonzero == 0:
                            continue
                        e = L[dy + 1, GROUPS + b, near, pl.ds(row + MAIN + dx, 8), :]
                        weight = 2.0 * 0.5 ** (nonzero - 1)
                        c = (scaled * weight) * (e / (own + e))
                        C[b * BLOCKS + t, l, (dl + 1) * 9 + (dx + 1) * 3 + dy + 1] = c
                        total = total + c
            C[b * BLOCKS + t, l, 13] = -total
            return carry

        lax.fori_loop(0, 2 * BLOCKS * LAYERS, one, 0)

    def advance():
        def one(it, carry):
            b = it // BLOCKS
            row = pl.multiple_of(lax.rem(it, BLOCKS) * 8, 8)
            group = pl.ds(b * 3, 3)
            acc = [None] * LAYERS

            def close(l):
                v = V[group, l, pl.ds(row, 8), :] + acc[l]
                V[group, l, pl.ds(row, 8), :] = v
                U[group, l, pl.ds(row, 8), :] = U[group, l, pl.ds(row, 8), :] + time_step * v

            for l in range(LAYERS):
                for dx in (-1, 0, 1):
                    for dy in (-1, 0, 1):
                        u = L[dy + 1, group, l, pl.ds(row + MAIN + dx, 8), :]
                        for dl in (-1, 0, 1):
                            target = l - dl
                            if not 0 <= target < LAYERS:
                                continue
                            c = C[it, target, (dl + 1) * 9 + (dx + 1) * 3 + dy + 1]
                            term = c[None] * u
                            acc[target] = term if acc[target] is None else acc[target] + term
                if l > 0:
                    close(l - 1)
            close(LAYERS - 1)
            return carry

        lax.fori_loop(0, 2 * BLOCKS, one, 0)

    def contact(step):
        def fetch(i, carry):
            for k in range(8):
                p = i * 8 + k
                ROWS[pl.ds(p, 1), :] = FACES[step, pl.ds(flat_s[p], 1), :]
            return carry

        lax.fori_loop(0, PAIRS // 8, fetch, 0)
        offsets = OFFS[...]
        shifted = cyclic_shift(ROWS[...], offsets, -1)
        projected = shifted + jnp.dot(
            shifted, mortar[...], precision=lax.Precision.HIGHEST, preferred_element_type=f32
        )
        slave = SL[...]
        gap = jnp.concatenate([slave, slave], axis=0) - projected
        traction = ACT[...] * jnp.maximum(0.0, -gap)
        SF[...] = traction[:TILE] + traction[TILE:]
        back = traction + lax.dot_general(
            traction, mortar[...], (((1,), (1,)), ((), ())),
            precision=lax.Precision.HIGHEST, preferred_element_type=f32,
        )
        part = cyclic_shift(back, offsets, 1)
        coarse = part.astype(jnp.bfloat16)
        fine = (part - coarse.astype(f32)).astype(jnp.bfloat16)
        return jnp.concatenate([coarse, fine], axis=1)

    def owner_sum(part, o):
        both = jnp.dot(OH[block_of(o), :], part, preferred_element_type=f32)
        return both[:, :TILE] + both[:, TILE:]

    def send_forces(step, part):
        sends = []
        for q in range(chips):
            o = 2 * lax.rem(chip + q, chips) + 1 - core
            T[block_of(o), :] = owner_sum(part, o)
            copy = remote(
                T.at[block_of(o)], RP.at[step, q], core_send.at[step, q], core_recv.at[step, q],
                at(gx, partner),
            )
            copy.start()
            sends.append(copy)
        for q in range(chips):
            o = mate(q)
            T[block_of(o), :] = owner_sum(part, o)
        return sends

    def forward_forces(step, sends):
        out = []
        for q in list(range(1, chips)) + [0]:
            o = mate(q)
            sends[q].wait_recv()
            T[block_of(o), :] = T[block_of(o), :] + RP[step, q]
            if q > 0:
                copy = remote(
                    T.at[block_of(o)], RR.at[step, q], sum_send.at[step, q], sum_recv.at[step, q],
                    at(gx, o),
                )
                copy.start()
                out.append(copy)
        return out

    def collect_forces(step, sends, out):
        for copy in out:
            copy.wait_recv()
        force = T[block_of(gy), :]
        for q in range(1, chips):
            force = force + RR[step, q]
        return force

    def push(group, force):
        v = V[group, 0] + force
        V[group, 0] = v
        U[group, 0] = U[group, 0] + time_step * force

    copies, own = send_faces(0, disp.at[MASTER, 0])
    loads[0].wait()
    loads[1].wait()
    pack(8)
    halos = halo_copies(0, 8)
    for copy in halos:
        copy.start()

    OFFS[...] = jnp.broadcast_to(pair_v[1:2, :], (TILE, PAIRS)).T
    ACT[...] = penalty_stiffness * jnp.broadcast_to(pair_v[2:3, :], (TILE, PAIRS)).T.astype(f32)

    def hot(i, carry):
        rows = pl.ds(pl.multiple_of(i * TILE, TILE), TILE)
        index = lax.broadcasted_iota(jnp.int32, (TILE, PAIRS), 0) + i * TILE
        OH[rows, :] = jnp.where(pair_v[0:1, :] == index, 1.0, 0.0).astype(jnp.bfloat16)
        return carry

    lax.fori_loop(0, n_gy, hot, 0)
    SL[...] = clear[...] + U[SLAVE, 0]
    loads[2].wait()
    DINV[...] = time_step / D[:, 0]

    for copy in halos:
        copy.wait_recv()
    spread(0, 0, 8)
    couplings()
    finish_faces(0, copies, own)
    part = contact(0)
    sends = send_forces(0, part)
    out = forward_forces(0, sends)
    loads[3].wait()
    advance()
    push(SLAVE, DINV[1] * SF[...])
    force = collect_forces(0, sends, out)
    push(MASTER, -DINV[0] * force)

    copies, own = send_faces(1, U.at[MASTER, 0])
    for copy in halos:
        copy.wait_send()
    pack(GROUPS)
    halos = halo_copies(1, GROUPS)
    for copy in halos:
        copy.start()
    SL[...] = clear[...] + U[SLAVE, 0]
    for copy in sends + out:
        copy.wait_send()
    for copy in halos:
        copy.wait_recv()
    spread(1, 0, GROUPS)
    finish_faces(1, copies, own)
    part = contact(1)
    sends = send_forces(1, part)
    out = forward_forces(1, sends)
    advance()
    push(SLAVE, DINV[1] * SF[...])

    def store(k, block):
        return [
            pltpu.make_async_copy(ref.at[block], res.at[block], store_sem.at[which, k])
            for which, (ref, res) in enumerate(((U, u_out), (V, v_out)))
        ]

    stores = store(0, (pl.ds(0, GROUPS), pl.ds(1, LAYERS - 1)))
    stores += store(1, (pl.ds(0, 2), 0)) + store(2, (pl.ds(3, 3), 0))
    for copy in stores:
        copy.start()
    force = collect_forces(1, sends, out)
    push(MASTER, -DINV[0] * force)
    last = store(3, (MASTER, 0))
    for copy in last:
        copy.start()
    for copy in sends + out + halos:
        copy.wait_send()
    for copy in stores + last:
        copy.wait()


def body(
    n_gx, n_gy, displacement, velocity, modulus, density, clearance, mortar_coupling,
    pair_owner, pair_row, pair_offset, pair_active,
):
    owners = pair_owner.reshape(TILE, 2)
    flat = owners * TILE + pair_row.reshape(TILE, 2)
    pairs = jnp.stack([flat, pair_offset.reshape(TILE, 2), pair_active.reshape(TILE, 2)])
    pairs = pairs.transpose(0, 2, 1).reshape(3, PAIRS)
    whole = (GROUPS, LAYERS, TILE, TILE)
    hbm = pl.BlockSpec(memory_space=pl.ANY)
    vmem = pl.BlockSpec(memory_space=pltpu.VMEM)
    smem = pl.BlockSpec(memory_space=pltpu.SMEM)
    chips = n_gy // 2
    dma = pltpu.SemaphoreType.DMA
    new_disp, new_vel = pl.pallas_call(
        functools.partial(kernel, n_gx, n_gy),
        out_shape=[jax.ShapeDtypeStruct(whole, f32)] * 2,
        in_specs=[hbm, hbm, hbm, hbm, vmem, vmem, smem, vmem],
        out_specs=[hbm, hbm],
        scratch_shapes=[
            pltpu.VMEM((8, LAYERS, TILE, TILE), f32),
            pltpu.VMEM(whole, f32),
            pltpu.VMEM((2, LAYERS, TILE, TILE), f32),
            pltpu.VMEM((3, 8, LAYERS, TILE + 16, TILE), f32),
            pltpu.VMEM((2 * BLOCKS, LAYERS, 27, 8, TILE), f32),
            pltpu.VMEM((STEPS, n_gy * TILE, TILE), f32),
            pltpu.VMEM((n_gy * TILE, TILE), f32),
            pltpu.VMEM((STEPS, chips, TILE, TILE), f32),
            pltpu.VMEM((STEPS, chips, TILE, TILE), f32),
            pltpu.VMEM((n_gy * TILE, PAIRS), jnp.bfloat16),
            pltpu.VMEM((2, 64, TILE), f32),
            pltpu.VMEM((2, 64, TILE), f32),
            pltpu.VMEM((STEPS, 2, 64, TILE), f32),
            pltpu.VMEM((STEPS, 2, 64, TILE), f32),
            pltpu.VMEM((STEPS, 4, 64, TILE), f32),
            pltpu.VMEM((PAIRS, TILE), jnp.int32),
            pltpu.VMEM((PAIRS, TILE), f32),
            pltpu.VMEM((TILE, TILE), f32),
            pltpu.VMEM((TILE, TILE), f32),
            pltpu.VMEM((PAIRS, TILE), f32),
            pltpu.VMEM((2, TILE, TILE), f32),
            dma((4,)),
            dma((STEPS,)),
            dma((STEPS, 8)), dma((STEPS, 8)),
            dma((STEPS, chips)), dma((STEPS, chips)),
            dma((STEPS, chips)), dma((STEPS, chips)),
            dma((STEPS, chips)), dma((STEPS, chips)),
            dma((STEPS, chips)), dma((STEPS, chips)),
            dma((2, 4)),
        ],
        compiler_params=pltpu.CompilerParams(
            collective_id=0, has_side_effects=True, vmem_limit_bytes=62 * 1024 * 1024
        ),
        name="impact",
    )(
        displacement.reshape(whole), velocity.reshape(whole), modulus, density,
        clearance, mortar_coupling, pairs[0], pairs,
    )
    shape = displacement.shape
    return new_disp.reshape(shape), new_vel.reshape(shape)


def solution(mesh):
    n_gx, n_gy = mesh.shape["gx"], mesh.shape["gy"]
    nodes = P(None, None, None, "gx", "gy")
    pairs = P("gx", "gy", None)
    return jax.shard_map(
        functools.partial(body, n_gx, n_gy),
        mesh=mesh,
        in_specs=(
            nodes, nodes, P(None, None, "gx", "gy"), P(None, None, "gx", "gy"), P("gx", "gy"), P(),
            pairs, pairs, pairs, pairs,
        ),
        out_specs=(nodes, nodes),
        check_vma=False,
    )
```

profile of v0, /device:TPU:1, one launch (start us, length us, event | category | flops | bytes accessed | tf_op | source)
XLA Modules:
  0.0 108.3 jit_solution(1554405763499299615)
XLA Ops:
  0.6 0.7 add_reduce_fusion
  1.3 0.5 broadcast.18
  1.9 1.3 %reduce.11 = s32[256]{0:T(256)S(1)} reduce(s32[1,256,1]{1,2,0:T(1,128)} %param.18, s32[]{:T(128)} %broadcast.18), dimensions={0,2}, to_apply=%param.18.reduce_sub_computation.3 | reduce | bytes 2052 | tf_op args[8]
  3.2 1.3 %reduce.10 = s32[256]{0:T(256)S(1)} reduce(s32[1,256,1]{1,2,0:T(1,128)} %param.19, s32[]{:T(128)} %broadcast.18), dimensions={0,2}, to_apply=%param.19.reduce_sub_computation.3 | reduce | bytes 2052 | tf_op args[9]
  4.5 0.1 stack_reshape.7
  4.7 0.1 copy.20
  4.7 0.2 stack_reshape.6
  4.9 0.1 copy.19
  5.0 0.2 add.14
  5.1 0.1 copy.18
  5.2 0.6 copy.23
  5.8 0.6 slice_bitcast_fusion.flat_s
  6.4 96.2 %impact.1 = (f32[6,8,128,128]{3,2,1,0:T(8,128)}, f32[6,8,128,128]{3,2,1,0:T(8,128)}) custom-call(f32[6,8,128,128]{3,2,1,0:T(8,128)} %bitcast.17, f32[6,8,128,128]{3,2,1,0:T(8,128)} %bitcast.18, f32[2,8,128,128]{3,2,1,0:T(8,128)} %mod.1, f32[2,8,128,128]{3,2,1,0:T(8,128)} %dens.1, f32[128,128]{1,0:T(8,128)} %clear.1, f32[128,128]{1,0:T(8,128)} %mortar.1, ...), custom_call_target="tpu_custom_call" | custom-call | tf_op jit(solution)/shard_map/impact/pallas_call | solution.py:429
  102.5 0.0 copy-start
  102.6 4.1 %copy.26 = f32[2,3,8,128,128]{4,3,2,1,0:T(8,128)} copy(f32[2,3,8,128,128]{4,3,2,1,0:T(8,128)} %bitcast.16) | data formatting | bytes 6291456
  106.6 0.0 copy-done
  106.6 1.7 %copy.27 = f32[2,3,8,128,128]{4,3,2,1,0:T(8,128)} copy(f32[2,3,8,128,128]{4,3,2,1,0:T(8,128)S(1)} %bitcast.15) | data formatting | bytes 6291456
  (1 shorter events, 0.0 us)
Async XLA Ops:
  102.5 4.1 %copy-start = (f32[6,8,128,128]{3,2,1,0:T(8,128)S(1)}, f32[6,8,128,128]{3,2,1,0:T(8,128)}, u32[]{:S(2)}) copy-start(f32[6,8,128,128]{3,2,1,0:T(8,128)} %get-tuple-element.5) | copy-start | bytes 9437188
where the time goes:
time: 109 us; the launch traced here: 108 us
  Pallas kernels  96.2 us (88%)
  local copies, waits for them, and re-layouts  8.05 us (7%)
  other arithmetic  3.4 us (3%)
    pallas_call x1, Pallas kernels, body(): pl.pallas_call(functools.partial(kernel, n_gx, n_gy), out_shape=[jax.Shap...  96.2 us
    unnamed x6, local copies, waits for them, and re-layouts  6.86 us
    unnamed x3, other arithmetic  2.69 us

commit v1 on v0

v1 whole, which is shorter than its diff:
```python
import functools

import jax
import jax.numpy as jnp
from jax import lax
from jax.experimental import pallas as pl
from jax.experimental.pallas import tpu as pltpu
from jax.sharding import PartitionSpec as P

STEPS = 2
LAYERS = 8
TILE = 128
BLOCKS = TILE // 8
PAIRS = 256
GROUPS = 6
MASTER, SLAVE = 2, 5
LOW, MAIN, HIGH = 7, 8, 136

time_step = 0.2
penalty_stiffness = 4.0

MESH = pl.DeviceIdType.MESH
f32 = jnp.float32


def lanes(shape):
    return lax.broadcasted_iota(jnp.int32, shape, len(shape) - 1)


def cyclic_shift(values, offsets, direction):
    for bit in range(7):
        amount = 1 << bit
        rolled = pltpu.roll(values, (direction * amount) % TILE, axis=1)
        values = jnp.where((offsets & amount) != 0, rolled, values)
    return values


def kernel(
    n_gx, n_gy,
    disp, vel, mod, dens, clear, mortar, owner_s, row_s, owner_v, row_v, offset_v, active_v,
    u_out, v_out,
    U, V, D, L, C, FACES, T, RP, RR, OH, XS, YS, HX, HY, HD, OFFS, ACT, SL, SF, ROWS, TR, DINV,
    load_sem, own_sem, halo_send, halo_recv, face_send, face_recv, pass_send, pass_recv,
    core_send, core_recv, sum_send, sum_recv, store_sem,
):
    gx = lax.axis_index("gx")
    gy = lax.axis_index("gy")
    core = lax.rem(gy, 2)
    chip = gy // 2
    chips = n_gy // 2
    partner = gy + 1 - 2 * core
    up = lax.rem(gx + n_gx - 1, n_gx)
    down = lax.rem(gx + 1, n_gx)
    left = lax.rem(gy + n_gy - 1, n_gy)
    right = lax.rem(gy + 1, n_gy)
    other = lax.rem(gy + n_gy - 1 + 2 * core, n_gy)

    def at(x, y):
        return {"gx": x, "gy": y}

    def mate(q):
        return 2 * lax.rem(chip + q, chips) + core

    loads = [
        pltpu.make_async_copy(disp, U.at[pl.ds(0, GROUPS)], load_sem.at[0]),
        pltpu.make_async_copy(mod, U.at[pl.ds(GROUPS, 2)], load_sem.at[1]),
        pltpu.make_async_copy(dens, D, load_sem.at[2]),
        pltpu.make_async_copy(vel, V, load_sem.at[3]),
    ]
    for load in loads:
        load.start()

    barrier = pltpu.get_barrier_semaphore()
    friends = [at(gx, mate(q)) for q in range(1, chips)]
    friends += [at(gx, partner), at(gx, other)]
    friends += [at(x, y) for x in (up, down) for y in (left, gy, right)]
    for friend in friends:
        pl.semaphore_signal(barrier, inc=1, device_id=friend, device_id_type=MESH)
    pl.semaphore_wait(barrier, len(friends))

    def remote(src, dst, send, recv, target):
        return pltpu.make_async_remote_copy(
            src_ref=src, dst_ref=dst, send_sem=send, recv_sem=recv,
            device_id=target, device_id_type=MESH,
        )

    def block_of(j):
        return pl.ds(pl.multiple_of(j * TILE, TILE), TILE)

    def face_copies(step, src):
        mine = FACES.at[step, block_of(gy)]
        out = [remote(src, mine, face_send.at[step, 0], face_recv.at[step, 0], at(gx, partner))]
        for q in range(1, chips):
            out.append(remote(src, mine, face_send.at[step, q], face_recv.at[step, q], at(gx, mate(q))))
        return out

    def pass_copy(step, q):
        held = FACES.at[step, block_of(mate(chips - q))]
        return remote(held, held, pass_send.at[step, q], pass_recv.at[step, q], at(gx, partner))

    def send_faces(step, src):
        copies = face_copies(step, src)
        for q in near + [0]:
            copies[q].start()
        own = pltpu.make_async_copy(src, FACES.at[step, block_of(gy)], own_sem.at[step])
        own.start()
        return copies, own

    near = [1, chips - 1] + list(range(2, chips - 1))

    def pass_faces(step, copies, order):
        passed = []
        for q in order:
            copies[q].wait_recv()
            copy = pass_copy(step, q)
            copy.start()
            passed.append(copy)
        return passed

    def finish_faces(copies, own, passed):
        own.wait()
        copies[0].wait_recv()
        for copy in passed:
            copy.wait_recv()
        for copy in copies + passed:
            copy.wait_send()

    def pack(first, groups):
        def one(i, carry):
            g = i // 2
            half = lax.rem(i, 2)
            lane = lanes((8, TILE)) // 2
            packed = jnp.zeros((8, TILE), f32)
            for t in range(4 * BLOCKS):
                tile = U[g, half * 4 + t // BLOCKS, t % BLOCKS * 8 : t % BLOCKS * 8 + 8, :]
                packed = jnp.where(lane == t, pltpu.roll(tile, 2 * t + 1, axis=1), packed)
            YS[pl.ds(pl.multiple_of(i * 8, 8), 8), :] = packed
            for k in range(4):
                l = half * 4 + k
                XS[0, pl.ds(g * 8 + l, 1), :] = U[g, l, 0:1, :]
                XS[1, pl.ds(g * 8 + l, 1), :] = U[g, l, TILE - 1 : TILE, :]
            return carry

        lax.fori_loop(2 * first, 2 * (first + groups), one, 0)

    def halo_copies(phase, step, first, groups):
        rows = pl.ds(first * 8, groups * 8)
        wide = pl.ds(first * 16, groups * 16)
        plan = [
            (XS.at[0, rows], HX.at[step, 1, rows], at(up, gy)),
            (XS.at[1, rows], HX.at[step, 0, rows], at(down, gy)),
            (YS.at[wide], HY.at[step, 1, wide], at(gx, left)),
            (YS.at[wide], HY.at[step, 0, wide], at(gx, right)),
            (XS.at[0, rows], HD.at[step, 3, rows], at(up, left)),
            (XS.at[0, rows], HD.at[step, 2, rows], at(up, right)),
            (XS.at[1, rows], HD.at[step, 1, rows], at(down, left)),
            (XS.at[1, rows], HD.at[step, 0, rows], at(down, right)),
        ]
        return [
            remote(src, dst, halo_send.at[phase, k], halo_recv.at[phase, k], target)
            for k, (src, dst, target) in enumerate(plan)
        ]

    def send_halos(phase, step, first, groups):
        pack(first, groups)
        copies = halo_copies(phase, step, first, groups)
        for copy in copies:
            copy.start()
        return copies

    def spread(step, first, groups):
        at_top = (gx == 0).astype(f32)
        at_bottom = (gx == n_gx - 1).astype(f32)
        at_left = (gy == 0).astype(f32)
        at_right = (gy == n_gy - 1).astype(f32)

        def one(g, carry):
            is_mod = (g >= GROUPS).astype(f32)
            keep_top, keep_bottom = 1.0 - is_mod * at_top, 1.0 - is_mod * at_bottom
            keep_left, keep_right = 1.0 - is_mod * at_left, 1.0 - is_mod * at_right
            lane = lanes((8, TILE))
            rows = pl.ds(pl.multiple_of(g * 8, 8), 8)

            def part(half, carry):
                wide = pl.ds(pl.multiple_of(g * 16 + half * 8, 8), 8)
                low = HY[step, 0, wide, :] * keep_left
                high = HY[step, 1, wide, :] * keep_right
                even = lane % 2 == 0
                both = jnp.where(even, pltpu.roll(high, TILE - 1, axis=1), pltpu.roll(low, 1, axis=1))
                for t in range(4 * BLOCKS):
                    l = half * 4 + t // BLOCKS
                    row = t % BLOCKS * 8
                    edge = pltpu.roll(both, TILE - 1 - 2 * t, axis=1)
                    here = U[g, l, row : row + 8, :]
                    into = slice(MAIN + row, MAIN + row + 8)
                    L[0, g, l, into, :] = jnp.where(lane == 0, edge, pltpu.roll(here, 1, axis=1))
                    L[1, g, l, into, :] = here
                    L[2, g, l, into, :] = jnp.where(lane == TILE - 1, edge, pltpu.roll(here, TILE - 1, axis=1))
                return carry

            lax.fori_loop(0, 2, part, 0)
            for side, keep, spot in ((0, keep_top, LOW), (1, keep_bottom, HIGH)):
                here = HX[step, side, rows, :] * keep
                corner_low = HD[step, 2 * side, rows, :] * (keep * keep_left)
                corner_high = HD[step, 2 * side + 1, rows, :] * (keep * keep_right)
                before = pltpu.roll(jnp.where(lane == TILE - 1, corner_low, here), 1, axis=1)
                after = pltpu.roll(jnp.where(lane == 0, corner_high, here), TILE - 1, axis=1)
                for dy, plane in enumerate((before, here, after)):
                    for l in range(LAYERS):
                        L[dy, g, l, spot : spot + 1, :] = plane[l : l + 1, :]
            return carry

        lax.fori_loop(first, first + groups, one, 0)

    def couplings(first, last):
        def one(it, carry):
            b = it // (BLOCKS // 2 * LAYERS)
            t = lax.rem(it // LAYERS, BLOCKS // 2)
            l = lax.rem(it, LAYERS)
            row = pl.multiple_of(t * 16, 16)
            own = L[1, GROUPS + b, l, pl.ds(row + MAIN, 16), :]
            base = own * ((2.0 * time_step) / D[b, l, pl.ds(row, 16), :])
            total = jnp.zeros((16, TILE), f32)
            for dl in (-1, 0, 1):
                near = jnp.clip(l + dl, 0, LAYERS - 1)
                inside = jnp.logical_and(l + dl >= 0, l + dl < LAYERS).astype(f32)
                scaled = base if dl == 0 else base * inside
                weights = [scaled, scaled * 0.5, scaled * 0.25] if dl else [None, scaled, scaled * 0.5]
                for dx in (-1, 0, 1):
                    for dy in (-1, 0, 1):
                        if dl == dx == dy == 0:
                            continue
                        e = L[dy + 1, GROUPS + b, near, pl.ds(row + MAIN + dx, 16), :]
                        c = weights[abs(dx) + abs(dy)] * (e * pl.reciprocal(own + e, approx=True))
                        C[b * (BLOCKS // 2) + t, l, (dl + 1) * 9 + (dx + 1) * 3 + dy + 1] = c
                        total = total + c
            C[b * (BLOCKS // 2) + t, l, 13] = -total
            return carry

        lax.fori_loop(first, last, one, 0)

    def advance(first, last):
        def one(it, carry):
            b = it // BLOCKS
            row = pl.multiple_of(lax.rem(it, BLOCKS) * 8, 8)
            odd = pl.multiple_of(lax.rem(it, 2) * 8, 8)
            group = pl.ds(b * 3, 3)
            acc = [None] * LAYERS

            def close(l):
                v = V[group, l, pl.ds(row, 8), :] + acc[l]
                V[group, l, pl.ds(row, 8), :] = v
                U[group, l, pl.ds(row, 8), :] = U[group, l, pl.ds(row, 8), :] + time_step * v

            for l in range(LAYERS):
                for dx in (-1, 0, 1):
                    for dy in (-1, 0, 1):
                        u = L[dy + 1, group, l, pl.ds(row + MAIN + dx, 8), :]
                        for dl in (-1, 0, 1):
                            target = l - dl
                            if not 0 <= target < LAYERS:
                                continue
                            c = C[it // 2, target, (dl + 1) * 9 + (dx + 1) * 3 + dy + 1, pl.ds(odd, 8)]
                            term = c[None] * u
                            acc[target] = term if acc[target] is None else acc[target] + term
                if l > 0:
                    close(l - 1)
            close(LAYERS - 1)
            return carry

        lax.fori_loop(first, last, one, 0)

    def contact(step):
        def fetch(i, carry):
            for k in range(8):
                p = i * 8 + k
                ROWS[pl.ds(p, 1), :] = FACES[step, pl.ds(owner_s[0, 0, p] * TILE + row_s[0, 0, p], 1), :]
            return carry

        lax.fori_loop(0, PAIRS // 8, fetch, 0)
        offsets = OFFS[...]
        shifted = cyclic_shift(ROWS[...], offsets, -1)
        projected = shifted + jnp.dot(
            shifted, mortar[...], precision=lax.Precision.HIGHEST, preferred_element_type=f32
        )
        traction = ACT[...] * jnp.maximum(0.0, projected - SL[...])
        TR[...] = traction
        SF[...] = TR[pl.ds(0, TILE, stride=2), :] + TR[pl.ds(1, TILE, stride=2), :]
        back = traction + lax.dot_general(
            traction, mortar[...], (((1,), (1,)), ((), ())),
            precision=lax.Precision.HIGHEST, preferred_element_type=f32,
        )
        part = cyclic_shift(back, offsets, 1)
        coarse = part.astype(jnp.bfloat16)
        fine = (part - coarse.astype(f32)).astype(jnp.bfloat16)
        return jnp.concatenate([coarse, fine], axis=1)

    def owner_sum(part, o):
        both = jnp.dot(OH[block_of(o), :], part, preferred_element_type=f32)
        return both[:, :TILE] + both[:, TILE:]

    def send_forces(step, part):
        sends = [None] * chips
        for q in near + [0]:
            o = 2 * lax.rem(chip + q, chips) + 1 - core
            T[block_of(o), :] = owner_sum(part, o)
            copy = remote(
                T.at[block_of(o)], RP.at[step, q], core_send.at[step, q], core_recv.at[step, q],
                at(gx, partner),
            )
            copy.start()
            sends[q] = copy
        for q in range(chips):
            o = mate(q)
            T[block_of(o), :] = owner_sum(part, o)
        return sends

    def forward_forces(step, sends, order):
        out = []
        for q in order:
            o = mate(q)
            sends[q].wait_recv()
            T[block_of(o), :] = T[block_of(o), :] + RP[step, q]
            if q > 0:
                copy = remote(
                    T.at[block_of(o)], RR.at[step, q], sum_send.at[step, q], sum_recv.at[step, q],
                    at(gx, o),
                )
                copy.start()
                out.append(copy)
        return out

    def collect_forces(step, out):
        for copy in out:
            copy.wait_recv()
        force = T[block_of(gy), :]
        for q in range(1, chips):
            force = force + RR[step, q]
        return force

    def push(group, force):
        v = V[group, 0] + force
        V[group, 0] = v
        U[group, 0] = U[group, 0] + time_step * force

    copies, own = send_faces(0, disp.at[MASTER, 0])
    loads[0].wait()
    loads[1].wait()
    halos = send_halos(0, 0, 0, 8)

    OFFS[...] = jnp.broadcast_to(offset_v[0], (TILE, PAIRS)).T
    ACT[...] = penalty_stiffness * jnp.broadcast_to(active_v[0], (TILE, PAIRS)).T.astype(f32)

    def hot(i, carry):
        rows = pl.ds(pl.multiple_of(i * TILE, TILE), TILE)
        index = lax.broadcasted_iota(jnp.int32, (TILE, PAIRS), 0) + i * TILE
        OH[rows, :] = jnp.where(owner_v[0] * TILE + row_v[0] == index, 1.0, 0.0).astype(jnp.bfloat16)
        return carry

    lax.fori_loop(0, n_gy, hot, 0)

    def slave_gaps():
        rest = clear[...] + U[SLAVE, 0]
        SL[pl.ds(0, TILE, stride=2), :] = rest
        SL[pl.ds(1, TILE, stride=2), :] = rest

    slave_gaps()
    for copy in halos:
        copy.wait_recv()
    spread(0, GROUPS, 2)
    passed = pass_faces(0, copies, near)
    spread(0, 0, GROUPS)
    finish_faces(copies, own, passed)
    part = contact(0)
    sends = send_forces(0, part)
    loads[2].wait()
    DINV[...] = time_step / D[:, 0]
    half = BLOCKS * LAYERS // 2
    couplings(0, half)
    out = forward_forces(0, sends, near + [0])
    couplings(half, 2 * half)
    loads[3].wait()
    advance(BLOCKS, 2 * BLOCKS)
    push(SLAVE, DINV[1] * SF[...])
    for copy in halos:
        copy.wait_send()
    halos = send_halos(1, 1, 3, 3)
    slave_gaps()
    advance(0, BLOCKS)
    force = collect_forces(0, out)
    push(MASTER, -DINV[0] * force)

    copies, own = send_faces(1, U.at[MASTER, 0])
    more = send_halos(2, 1, 0, 3)
    for copy in sends + out:
        copy.wait_send()
    for copy in halos:
        copy.wait_recv()
    spread(1, 3, 3)
    for copy in more:
        copy.wait_recv()
    spread(1, 0, 3)
    passed = pass_faces(1, copies, near)
    finish_faces(copies, own, passed)
    part = contact(1)
    sends = send_forces(1, part)
    advance(0, 4)
    out = []
    for k, q in enumerate(near):
        advance(4 + 2 * k, 6 + 2 * k)
        out += forward_forces(1, sends, [q])
    forward_forces(1, sends, [0])
    advance(2 + 2 * chips, 2 * BLOCKS)
    push(SLAVE, DINV[1] * SF[...])

    def store(k, block):
        return [
            pltpu.make_async_copy(ref.at[block], res.at[block], store_sem.at[which, k])
            for which, (ref, res) in enumerate(((U, u_out), (V, v_out)))
        ]

    stores = store(0, (pl.ds(0, GROUPS), pl.ds(1, LAYERS - 1)))
    stores += store(1, (pl.ds(0, 2), 0)) + store(2, (pl.ds(3, 3), 0))
    for copy in stores:
        copy.start()
    force = collect_forces(1, out)
    push(MASTER, -DINV[0] * force)
    last = store(3, (MASTER, 0))
    for copy in last:
        copy.start()
    for copy in sends + out + halos + more:
        copy.wait_send()
    for copy in stores + last:
        copy.wait()


def body(
    n_gx, n_gy, displacement, velocity, modulus, density, clearance, mortar_coupling,
    pair_owner, pair_row, pair_offset, pair_active,
):
    owner, row, offset, active = (
        x.transpose(0, 2, 1) for x in (pair_owner, pair_row, pair_offset, pair_active)
    )
    whole = (GROUPS, LAYERS, TILE, TILE)
    hbm = pl.BlockSpec(memory_space=pl.ANY)
    vmem = pl.BlockSpec(memory_space=pltpu.VMEM)
    smem = pl.BlockSpec(memory_space=pltpu.SMEM)
    chips = n_gy // 2
    dma = pltpu.SemaphoreType.DMA
    new_disp, new_vel = pl.pallas_call(
        functools.partial(kernel, n_gx, n_gy),
        out_shape=[jax.ShapeDtypeStruct(whole, f32)] * 2,
        in_specs=[hbm] * 4 + [vmem] * 2 + [smem] * 2 + [vmem] * 4,
        out_specs=[hbm, hbm],
        scratch_shapes=[
            pltpu.VMEM((8, LAYERS, TILE, TILE), f32),
            pltpu.VMEM(whole, f32),
            pltpu.VMEM((2, LAYERS, TILE, TILE), f32),
            pltpu.VMEM((3, 8, LAYERS, TILE + 16, TILE), f32),
            pltpu.VMEM((BLOCKS, LAYERS, 27, 16, TILE), f32),
            pltpu.VMEM((STEPS, n_gy * TILE, TILE), f32),
            pltpu.VMEM((n_gy * TILE, TILE), f32),
            pltpu.VMEM((STEPS, chips, TILE, TILE), f32),
            pltpu.VMEM((STEPS, chips, TILE, TILE), f32),
            pltpu.VMEM((n_gy * TILE, PAIRS), jnp.bfloat16),
            pltpu.VMEM((2, 64, TILE), f32),
            pltpu.VMEM((128, TILE), f32),
            pltpu.VMEM((STEPS, 2, 64, TILE), f32),
            pltpu.VMEM((STEPS, 2, 128, TILE), f32),
            pltpu.VMEM((STEPS, 4, 64, TILE), f32),
            pltpu.VMEM((PAIRS, TILE), jnp.int32),
            pltpu.VMEM((PAIRS, TILE), f32),
            pltpu.VMEM((PAIRS, TILE), f32),
            pltpu.VMEM((TILE, TILE), f32),
            pltpu.VMEM((PAIRS, TILE), f32),
            pltpu.VMEM((PAIRS, TILE), f32),
            pltpu.VMEM((2, TILE, TILE), f32),
            dma((4,)),
            dma((STEPS,)),
            dma((3, 8)), dma((3, 8)),
            dma((STEPS, chips)), dma((STEPS, chips)),
            dma((STEPS, chips)), dma((STEPS, chips)),
            dma((STEPS, chips)), dma((STEPS, chips)),
            dma((STEPS, chips)), dma((STEPS, chips)),
            dma((2, 4)),
        ],
        compiler_params=pltpu.CompilerParams(
            collective_id=0, has_side_effects=True, vmem_limit_bytes=62 * 1024 * 1024
        ),
        name="impact",
    )(
        displacement.reshape(whole), velocity.reshape(whole), modulus, density,
        clearance, mortar_coupling, owner, row, owner, row, offset, active,
    )
    shape = displacement.shape
    return new_disp.reshape(shape), new_vel.reshape(shape)


def solution(mesh):
    n_gx, n_gy = mesh.shape["gx"], mesh.shape["gy"]
    nodes = P(None, None, None, "gx", "gy")
    pairs = P("gx", "gy", None)
    return jax.shard_map(
        functools.partial(body, n_gx, n_gy),
        mesh=mesh,
        in_specs=(
            nodes, nodes, P(None, None, "gx", "gy"), P(None, None, "gx", "gy"), P("gx", "gy"), P(),
            pairs, pairs, pairs, pairs,
        ),
        out_specs=(nodes, nodes),
        check_vma=False,
    )
```

time: 109 us -> 82.3 us (0.76)
  Pallas kernels: 96.2 us -> 75.8 us
  other arithmetic: 3.4 us -> 0 us
  local copies, waits for them, and re-layouts: 8.05 us -> 5.73 us
    pallas_call x1, Pallas kernels: 96.2 us -> 75.8 us  [body(): pl.pallas_call(functools.partial(kernel, n_gx, n_gy), out_shape=[jax.Shap...]
    unnamed x3 -> x0, other arithmetic: 2.69 us -> none
    unnamed x6 -> x4, local copies, waits for them, and re-layouts: 6.86 us -> 5.73 us
where the time goes in v1:
time: 82.3 us; the launch traced here: 82.1 us
  Pallas kernels  75.8 us (92%)
  local copies, waits for them, and re-layouts  5.73 us (7%)
    pallas_call x1, Pallas kernels, body(): pl.pallas_call(functools.partial(kernel, n_gx, n_gy), out_shape=[jax.Shap...  75.8 us
    unnamed x4, local copies, waits for them, and re-layouts  5.73 us

profile of v1, /device:TPU:1, one launch (start us, length us, event | category | flops | bytes accessed | tf_op | source)
XLA Modules:
  0.0 82.1 jit_solution(4245311306489976752)
XLA Ops:
  0.6 75.8 %impact.1 = (f32[6,8,128,128]{3,2,1,0:T(8,128)}, f32[6,8,128,128]{3,2,1,0:T(8,128)}) custom-call(f32[6,8,128,128]{3,2,1,0:T(8,128)} %bitcast.8, f32[6,8,128,128]{3,2,1,0:T(8,128)} %bitcast.9, f32[2,8,128,128]{3,2,1,0:T(8,128)} %mod.1, f32[2,8,128,128]{3,2,1,0:T(8,128)} %dens.1, f32[128,128]{1,0:T(8,128)} %clear.1, f32[128,128]{1,0:T(8,128)} %mortar.1, ...), custom_call_target="tpu_custom_call" | custom-call | tf_op jit(solution)/shard_map/impact/pallas_call | solution.py:450
  76.4 0.0 copy-start
  76.4 4.1 %copy.14 = f32[2,3,8,128,128]{4,3,2,1,0:T(8,128)} copy(f32[2,3,8,128,128]{4,3,2,1,0:T(8,128)} %bitcast.11) | data formatting | bytes 6291456
  80.5 0.0 copy-done
  80.5 1.7 %copy.15 = f32[2,3,8,128,128]{4,3,2,1,0:T(8,128)} copy(f32[2,3,8,128,128]{4,3,2,1,0:T(8,128)S(1)} %bitcast.10) | data formatting | bytes 6291456
Async XLA Ops:
  76.4 4.1 %copy-start = (f32[6,8,128,128]{3,2,1,0:T(8,128)S(1)}, f32[6,8,128,128]{3,2,1,0:T(8,128)}, u32[]{:S(2)}) copy-start(f32[6,8,128,128]{3,2,1,0:T(8,128)} %get-tuple-element.5) | copy-start | bytes 9437188

commit v2 on v1

v2 whole, which is shorter than its diff:
```python
import functools

import jax
import jax.numpy as jnp
from jax import lax
from jax.experimental import pallas as pl
from jax.experimental.pallas import tpu as pltpu
from jax.sharding import PartitionSpec as P

STEPS = 2
LAYERS = 8
TILE = 128
BLOCKS = TILE // 8
PAIRS = 256
GROUPS = 6
MASTER, SLAVE = 2, 5
LOW, MAIN, HIGH = 7, 8, 136

time_step = 0.2
penalty_stiffness = 4.0

VMEM_LIMIT = 62 * 1024 * 1024

MESH = pl.DeviceIdType.MESH
f32 = jnp.float32


def lanes(shape):
    return lax.broadcasted_iota(jnp.int32, shape, len(shape) - 1)


def cyclic_shift(values, offsets, direction):
    for bit in range(7):
        amount = 1 << bit
        rolled = pltpu.roll(values, (direction * amount) % TILE, axis=1)
        values = jnp.where((offsets & amount) != 0, rolled, values)
    return values


def kernel(
    n_gx, n_gy,
    disp, vel, mod, dens, clear, mortar, owner_s, row_s, owner_v, row_v, offset_v, active_v,
    u_out, v_out,
    U, V, E, D, L, C, FACES, T, PART, RR, OH, FLAT, XS, YS, CS, HX, HY, HD, OFFS, ACT, SL, SF, ROWS, TR, DINV,
    load_sem, own_sem, halo_send, halo_recv, face_send, face_recv, pass_send, pass_recv,
    core_send, core_recv, sum_send, sum_recv, store_sem,
):
    gx = lax.axis_index("gx")
    gy = lax.axis_index("gy")
    core = lax.rem(gy, 2)
    plane = n_gy // 2
    ring = n_gy // 4
    partner = gy + 1 - 2 * core
    up = lax.rem(gx + n_gx - 1, n_gx)
    down = lax.rem(gx + 1, n_gx)
    left = lax.rem(gy + n_gy - 1, n_gy)
    right = lax.rem(gy + 1, n_gy)
    other = lax.rem(gy + n_gy - 1 + 2 * core, n_gy)

    def at(x, y):
        return {"gx": x, "gy": y}

    def mate(dz, dy):
        z = lax.rem(gy // plane + dz, 2)
        y = lax.rem(lax.rem(gy, plane) // 2 + dy, ring)
        return z * plane + 2 * y + core

    loads = [
        pltpu.make_async_copy(disp, U, load_sem.at[0]),
        pltpu.make_async_copy(mod, E, load_sem.at[1]),
        pltpu.make_async_copy(dens, D, load_sem.at[2]),
        pltpu.make_async_copy(vel, V, load_sem.at[3]),
    ]
    for load in loads:
        load.start()

    barrier = pltpu.get_barrier_semaphore()
    friends = [at(gx, mate(*d)) for d in ((0, 1), (0, 2), (0, 3), (1, 0))]
    friends += [at(gx, partner), at(gx, other)]
    friends += [at(x, y) for x in (up, down) for y in (left, gy, right)]
    for friend in friends:
        pl.semaphore_signal(barrier, inc=1, device_id=friend, device_id_type=MESH)
    pl.semaphore_wait(barrier, len(friends))

    def remote(src, dst, send, recv, target):
        return pltpu.make_async_remote_copy(
            src_ref=src, dst_ref=dst, send_sem=send, recv_sem=recv,
            device_id=target, device_id_type=MESH,
        )

    def block_of(j):
        return pl.ds(pl.multiple_of(j * TILE, TILE), TILE)

    def relay(step, dz, dy, k, target):
        held = FACES.at[step, block_of(mate(dz, dy))]
        return remote(held, held, face_send.at[step, k], face_recv.at[step, k], at(gx, target))

    def send_faces(step, src):
        mine = FACES.at[step, block_of(gy)]
        copies = {}
        for k, target in ((4, mate(1, 0)), (2, mate(0, 2)), (1, mate(0, 3)), (3, mate(0, 1)), (0, partner)):
            copies[k] = remote(src, mine, face_send.at[step, k], face_recv.at[step, k], at(gx, target))
            copies[k].start()
        own = pltpu.make_async_copy(src, mine, own_sem.at[step])
        own.start()
        return copies, own

    def share(step, copies, k):
        copies[k].wait_recv()
        held = FACES.at[step, block_of(mate(k // 4, k % 4))]
        copies[8 + k] = remote(held, held, pass_send.at[step, k], pass_recv.at[step, k], at(gx, partner))
        copies[8 + k].start()

    def relay_faces(step, copies):
        share(step, copies, 4)
        copies[5] = relay(step, 1, 0, 5, mate(0, 3))
        copies[7] = relay(step, 1, 0, 7, mate(0, 1))
        copies[5].start()
        copies[7].start()
        share(step, copies, 2)
        copies[6] = relay(step, 0, 2, 6, mate(1, 0))
        copies[6].start()

    def finish_faces(step, copies, own):
        for k in (1, 3, 5, 7, 6):
            share(step, copies, k)
        own.wait()
        copies[0].wait_recv()
        for k in range(1, 8):
            copies[8 + k].wait_recv()
        for k in copies:
            copies[k].wait_send()

    def pack(phase, src, base, first, groups):
        def one(g, carry):
            lane = lanes((8, TILE))
            halves = []
            for half in range(2):
                packed = jnp.zeros((8, TILE), f32)
                for t in range(4 * BLOCKS):
                    tile = src[g - base, half * 4 + t // BLOCKS, t % BLOCKS * 8 : t % BLOCKS * 8 + 8, :]
                    packed = jnp.where(lane // 2 == t, pltpu.roll(tile, 2 * t + 1, axis=1), packed)
                halves.append(packed)
            even = lane % 2 == 0
            to_right = jnp.where(even, halves[0], pltpu.roll(halves[1], 1, axis=1))
            to_left = jnp.where(even, pltpu.roll(halves[1], TILE - 1, axis=1), halves[0])
            rows = pl.ds(pl.multiple_of(g * 8, 8), 8)
            for side, columns in enumerate((to_left, to_right)):
                YS[side, rows, :] = columns
                CS[phase, side, pl.ds(g, 1), :] = columns[0:1, :]
                CS[phase, 2 + side, pl.ds(g, 1), :] = columns[7:8, :]
            for l in range(LAYERS):
                XS[0, pl.ds(g * 8 + l, 1), :] = src[g - base, l, 0:1, :]
                XS[1, pl.ds(g * 8 + l, 1), :] = src[g - base, l, TILE - 1 : TILE, :]
            return carry

        lax.fori_loop(first, first + groups, one, 0)

    def halo_copies(phase, first, groups):
        step = 1 if phase in (1, 2) else 0
        rows = pl.ds(first * 8, groups * 8)
        plan = [
            (XS.at[0, rows], HX.at[step, 1, rows], at(up, gy)),
            (XS.at[1, rows], HX.at[step, 0, rows], at(down, gy)),
            (YS.at[0, rows], HY.at[step, 1, rows], at(gx, left)),
            (YS.at[1, rows], HY.at[step, 0, rows], at(gx, right)),
            (CS.at[phase, 0], HD.at[phase, 3], at(up, left)),
            (CS.at[phase, 1], HD.at[phase, 2], at(up, right)),
            (CS.at[phase, 2], HD.at[phase, 1], at(down, left)),
            (CS.at[phase, 3], HD.at[phase, 0], at(down, right)),
        ]
        return [
            remote(src, dst, halo_send.at[phase, k], halo_recv.at[phase, k], target)
            for k, (src, dst, target) in enumerate(plan)
        ]

    def send_halos(phase, src, base, first, groups):
        pack(phase, src, base, first, groups)
        copies = halo_copies(phase, first, groups)
        for copy in copies:
            copy.start()
        return copies

    def spread(phase, src, base, first, groups):
        step = 1 if phase in (1, 2) else 0
        at_top = (gx == 0).astype(f32)
        at_bottom = (gx == n_gx - 1).astype(f32)
        at_left = (gy == 0).astype(f32)
        at_right = (gy == n_gy - 1).astype(f32)

        def one(g, carry):
            is_mod = (g >= GROUPS).astype(f32)
            keep_top, keep_bottom = 1.0 - is_mod * at_top, 1.0 - is_mod * at_bottom
            keep_left, keep_right = 1.0 - is_mod * at_left, 1.0 - is_mod * at_right
            lane = lanes((8, TILE))
            rows = pl.ds(pl.multiple_of(g * 8, 8), 8)

            low = HY[step, 0, rows, :] * keep_left
            high = HY[step, 1, rows, :] * keep_right
            even = lane % 2 == 0
            for half in range(2):
                if half == 0:
                    both = jnp.where(even, pltpu.roll(high, TILE - 1, axis=1), pltpu.roll(low, 1, axis=1))
                else:
                    both = jnp.where(even, high, low)
                for t in range(4 * BLOCKS):
                    l = half * 4 + t // BLOCKS
                    row = t % BLOCKS * 8
                    edge = pltpu.roll(both, TILE - 1 - 2 * t, axis=1)
                    here = src[g - base, l, row : row + 8, :]
                    into = slice(MAIN + row, MAIN + row + 8)
                    L[0, g, l, into, :] = jnp.where(lane == 0, edge, pltpu.roll(here, 1, axis=1))
                    L[1, g, l, into, :] = here
                    L[2, g, l, into, :] = jnp.where(lane == TILE - 1, edge, pltpu.roll(here, TILE - 1, axis=1))
            layer = lax.broadcasted_iota(jnp.int32, (LAYERS, TILE), 0)
            upper = layer // 4

            def corner(k, block, flip):
                spot = 32 * (layer % 4) + 2 * block + (1 - upper if flip else upper)
                row = jnp.broadcast_to(HD[phase, k, pl.ds(g, 1), :], (LAYERS, TILE))
                return jnp.sum(jnp.where(lane == spot, row, 0.0), axis=1, keepdims=True)

            for side, keep, spot in ((0, keep_top, LOW), (1, keep_bottom, HIGH)):
                here = HX[step, side, rows, :] * keep
                block = 0 if side else BLOCKS - 1
                corner_low = corner(2 * side, block, False) * (keep * keep_left)
                corner_high = corner(2 * side + 1, block, True) * (keep * keep_right)
                before = pltpu.roll(jnp.where(lane == TILE - 1, corner_low, here), 1, axis=1)
                after = pltpu.roll(jnp.where(lane == 0, corner_high, here), TILE - 1, axis=1)
                for dy, plane in enumerate((before, here, after)):
                    for l in range(LAYERS):
                        L[dy, g, l, spot : spot + 1, :] = plane[l : l + 1, :]
            return carry

        lax.fori_loop(first, first + groups, one, 0)

    def couplings(first, last):
        def one(it, carry):
            b = it // (BLOCKS // 2 * LAYERS)
            t = lax.rem(it // LAYERS, BLOCKS // 2)
            l = lax.rem(it, LAYERS)
            row = pl.multiple_of(t * 16, 16)
            own = L[1, GROUPS + b, l, pl.ds(row + MAIN, 16), :]
            base = own * ((2.0 * time_step) / D[b, l, pl.ds(row, 16), :])
            total = jnp.zeros((16, TILE), f32)
            for dl in (-1, 0, 1):
                near = jnp.clip(l + dl, 0, LAYERS - 1)
                inside = jnp.logical_and(l + dl >= 0, l + dl < LAYERS).astype(f32)
                scaled = base if dl == 0 else base * inside
                weights = [scaled, scaled * 0.5, scaled * 0.25] if dl else [None, scaled, scaled * 0.5]
                for dx in (-1, 0, 1):
                    for dy in (-1, 0, 1):
                        if dl == dx == dy == 0:
                            continue
                        e = L[dy + 1, GROUPS + b, near, pl.ds(row + MAIN + dx, 16), :]
                        c = weights[abs(dx) + abs(dy)] * (e * pl.reciprocal(own + e, approx=True))
                        C[b * (BLOCKS // 2) + t, l, (dl + 1) * 9 + (dx + 1) * 3 + dy + 1] = c
                        total = total + c
            C[b * (BLOCKS // 2) + t, l, 13] = -total
            return carry

        lax.fori_loop(first, last, one, 0)

    def advance(first, last):
        def one(it, carry):
            b = it // BLOCKS
            row = pl.multiple_of(lax.rem(it, BLOCKS) * 8, 8)
            odd = pl.multiple_of(lax.rem(it, 2) * 8, 8)
            group = pl.ds(b * 3, 3)
            acc = [None] * LAYERS

            def close(l):
                v = V[group, l, pl.ds(row, 8), :] + acc[l]
                V[group, l, pl.ds(row, 8), :] = v
                U[group, l, pl.ds(row, 8), :] = U[group, l, pl.ds(row, 8), :] + time_step * v

            for l in range(LAYERS):
                for dx in (-1, 0, 1):
                    for dy in (-1, 0, 1):
                        u = L[dy + 1, group, l, pl.ds(row + MAIN + dx, 8), :]
                        for dl in (-1, 0, 1):
                            target = l - dl
                            if not 0 <= target < LAYERS:
                                continue
                            c = C[it // 2, target, (dl + 1) * 9 + (dx + 1) * 3 + dy + 1, pl.ds(odd, 8)]
                            term = c[None] * u
                            acc[target] = term if acc[target] is None else acc[target] + term
                if l > 0:
                    close(l - 1)
            close(LAYERS - 1)
            return carry

        lax.fori_loop(first, last, one, 0)

    def contact(step):
        def fetch(i, carry):
            for k in range(8):
                p = i * 8 + k
                ROWS[pl.ds(p, 1), :] = FACES[step, pl.ds(owner_s[0, 0, p] * TILE + row_s[0, 0, p], 1), :]
            return carry

        lax.fori_loop(0, PAIRS // 8, fetch, 0)
        offsets = OFFS[...]
        shifted = cyclic_shift(ROWS[...], offsets, -1)
        projected = shifted + jnp.dot(
            shifted, mortar[...], precision=lax.Precision.HIGHEST, preferred_element_type=f32
        )
        traction = ACT[...] * jnp.maximum(0.0, projected - SL[...])
        TR[...] = traction
        SF[...] = TR[pl.ds(0, TILE, stride=2), :] + TR[pl.ds(1, TILE, stride=2), :]
        back = traction + lax.dot_general(
            traction, mortar[...], (((1,), (1,)), ((), ())),
            precision=lax.Precision.HIGHEST, preferred_element_type=f32,
        )
        PART[step, 0] = cyclic_shift(back, offsets, 1)
        copy = remote(PART.at[step, 0], PART.at[step, 1], core_send.at[step], core_recv.at[step], at(gx, partner))
        copy.start()
        return copy

    order = ((1, 1), (1, 3), (1, 2), (0, 1), (0, 3), (1, 0), (0, 2), (0, 0))

    def split(values):
        coarse = values.astype(jnp.bfloat16)
        return jnp.concatenate([coarse, (values - coarse.astype(f32)).astype(jnp.bfloat16)], axis=1)

    def rows_of(there):
        return block_of(mate(*there) // 2)

    def first_sums(step, exchange):
        exchange.wait_recv()
        part = jnp.concatenate([split(PART[step, 0]), split(PART[step, 1])], axis=0)
        targets = ((0, 1), (0, 3), (1, 0), (0, 1), (0, 3))
        out = []
        for k, there in enumerate(order):
            rows = rows_of(there)
            both = jnp.dot(OH[rows, :], part, preferred_element_type=f32)
            T[rows, :] = both[:, :TILE] + both[:, TILE:]
            if k < len(targets):
                out.append(send_sum(step, there, k, targets[k]))
        return out

    def send_sum(step, there, k, target):
        copy = remote(
            T.at[rows_of(there)], RR.at[step, k], sum_send.at[step, k], sum_recv.at[step, k],
            at(gx, mate(*target)),
        )
        copy.start()
        return copy

    def second_sums(step, out):
        out[0].wait_recv()
        out[1].wait_recv()
        rows = rows_of((1, 0))
        T[rows, :] = T[rows, :] + RR[step, 0] + RR[step, 1]
        out.append(send_sum(step, (1, 0), 5, (1, 0)))
        out[2].wait_recv()
        rows = rows_of((0, 2))
        T[rows, :] = T[rows, :] + RR[step, 2]
        out.append(send_sum(step, (0, 2), 6, (0, 2)))

    def collect_forces(step, out):
        force = T[rows_of((0, 0)), :]
        for k in (3, 4, 6, 5):
            out[k].wait_recv()
            force = force + RR[step, k]
        return force

    def push(group, force):
        v = V[group, 0] + force
        V[group, 0] = v
        U[group, 0] = U[group, 0] + time_step * force

    copies, own = send_faces(0, disp.at[MASTER, 0])
    FLAT[0] = jnp.broadcast_to(owner_v[0] * TILE + row_v[0], (8, PAIRS))
    indices = remote(FLAT.at[0], FLAT.at[1], core_send.at[2], core_recv.at[2], at(gx, partner))
    indices.start()
    loads[1].wait()
    stiff = send_halos(3, E, GROUPS, GROUPS, 2)
    loads[0].wait()
    halos = send_halos(0, U, 0, 0, GROUPS)

    OFFS[...] = jnp.broadcast_to(offset_v[0], (TILE, PAIRS)).T
    ACT[...] = penalty_stiffness * jnp.broadcast_to(active_v[0], (TILE, PAIRS)).T.astype(f32)
    indices.wait_recv()

    def hot(m, carry):
        rows = pl.ds(pl.multiple_of(m * TILE, TILE), TILE)
        index = lax.broadcasted_iota(jnp.int32, (TILE, PAIRS), 0) + (2 * m + core) * TILE
        for side in range(2):
            OH[rows, side * PAIRS : (side + 1) * PAIRS] = jnp.where(
                FLAT[side, 0:1, :] == index, 1.0, 0.0
            ).astype(jnp.bfloat16)
        return carry

    lax.fori_loop(0, n_gy // 2, hot, 0)

    def slave_gaps():
        rest = clear[...] + U[SLAVE, 0]
        SL[pl.ds(0, TILE, stride=2), :] = rest
        SL[pl.ds(1, TILE, stride=2), :] = rest

    slave_gaps()
    relay_faces(0, copies)
    for copy in stiff:
        copy.wait_recv()
    spread(3, E, GROUPS, GROUPS, 2)
    loads[2].wait()
    DINV[...] = time_step / D[:, 0]
    half = BLOCKS * LAYERS // 2
    couplings(0, half)
    finish_faces(0, copies, own)
    exchange = contact(0)
    for copy in halos:
        copy.wait_recv()
    spread(0, U, 0, 0, 3)
    out = first_sums(0, exchange)
    spread(0, U, 0, 3, 3)
    loads[3].wait()
    advance(0, BLOCKS)
    second_sums(0, out)
    couplings(half, 2 * half)
    force = collect_forces(0, out)
    push(MASTER, -DINV[0] * force)

    copies, own = send_faces(1, U.at[MASTER, 0])
    for copy in halos + stiff:
        copy.wait_send()
    halos = send_halos(1, U, 0, 0, 3)
    advance(BLOCKS, 2 * BLOCKS)
    push(SLAVE, DINV[1] * SF[...])
    more = send_halos(2, U, 0, 3, 3)
    relay_faces(1, copies)
    slave_gaps()
    for copy in out:
        copy.wait_send()
    exchange.wait_send()
    for copy in halos:
        copy.wait_recv()
    spread(1, U, 0, 0, 3)
    for copy in more:
        copy.wait_recv()
    spread(2, U, 0, 3, 3)
    finish_faces(1, copies, own)
    exchange = contact(1)
    advance(0, 4)
    out = first_sums(1, exchange)
    advance(4, BLOCKS + 8)
    second_sums(1, out)
    advance(BLOCKS + 8, 2 * BLOCKS)
    push(SLAVE, DINV[1] * SF[...])

    def store(k, block):
        copies = [
            pltpu.make_async_copy(ref.at[block], res.at[block], store_sem.at[which, k])
            for which, (ref, res) in enumerate(((U, u_out), (V, v_out)))
        ]
        for copy in copies:
            copy.start()
        return copies

    stores = store(0, (pl.ds(0, GROUPS), pl.ds(1, LAYERS - 1)))
    stores += store(1, (pl.ds(0, 2), 0)) + store(2, (pl.ds(3, 3), 0))
    force = collect_forces(1, out)
    push(MASTER, -DINV[0] * force)
    stores += store(3, (MASTER, 0))
    indices.wait_send()
    exchange.wait_send()
    for copy in out + halos + more:
        copy.wait_send()
    for copy in stores:
        copy.wait()


def body(
    n_gx, n_gy, displacement, velocity, modulus, density, clearance, mortar_coupling,
    pair_owner, pair_row, pair_offset, pair_active,
):
    owner, row, offset, active = (
        x.transpose(0, 2, 1) for x in (pair_owner, pair_row, pair_offset, pair_active)
    )
    whole = (GROUPS, LAYERS, TILE, TILE)
    hbm = pl.BlockSpec(memory_space=pl.ANY)
    vmem = pl.BlockSpec(memory_space=pltpu.VMEM)
    smem = pl.BlockSpec(memory_space=pltpu.SMEM)
    chips = n_gy // 2
    dma = pltpu.SemaphoreType.DMA
    new_disp, new_vel = pl.pallas_call(
        functools.partial(kernel, n_gx, n_gy),
        out_shape=[jax.ShapeDtypeStruct(whole, f32)] * 2,
        in_specs=[hbm] * 4 + [vmem] * 2 + [smem] * 2 + [vmem] * 4,
        out_specs=[hbm, hbm],
        scratch_shapes=[
            pltpu.VMEM(whole, f32),
            pltpu.VMEM(whole, f32),
            pltpu.VMEM((2, LAYERS, TILE, TILE), f32),
            pltpu.VMEM((2, LAYERS, TILE, TILE), f32),
            pltpu.VMEM((3, 8, LAYERS, TILE + 16, TILE), f32),
            pltpu.VMEM((BLOCKS, LAYERS, 27, 16, TILE), f32),
            pltpu.VMEM((STEPS, n_gy * TILE, TILE), f32),
            pltpu.VMEM((n_gy * TILE // 2, TILE), f32),
            pltpu.VMEM((STEPS, 2, PAIRS, TILE), f32),
            pltpu.VMEM((STEPS, chips, TILE, TILE), f32),
            pltpu.VMEM((n_gy * TILE // 2, 2 * PAIRS), jnp.bfloat16),
            pltpu.VMEM((2, 8, PAIRS), jnp.int32),
            pltpu.VMEM((2, 64, TILE), f32),
            pltpu.VMEM((2, 64, TILE), f32),
            pltpu.VMEM((4, 4, 8, TILE), f32),
            pltpu.VMEM((STEPS, 2, 64, TILE), f32),
            pltpu.VMEM((STEPS, 2, 64, TILE), f32),
            pltpu.VMEM((4, 4, 8, TILE), f32),
            pltpu.VMEM((PAIRS, TILE), jnp.int32),
            pltpu.VMEM((PAIRS, TILE), f32),
            pltpu.VMEM((PAIRS, TILE), f32),
            pltpu.VMEM((TILE, TILE), f32),
            pltpu.VMEM((PAIRS, TILE), f32),
            pltpu.VMEM((PAIRS, TILE), f32),
            pltpu.VMEM((2, TILE, TILE), f32),
            dma((4,)),
            dma((STEPS,)),
            dma((4, 8)), dma((4, 8)),
            dma((STEPS, chips)), dma((STEPS, chips)),
            dma((STEPS, chips)), dma((STEPS, chips)),
            dma((3,)), dma((3,)),
            dma((STEPS, chips)), dma((STEPS, chips)),
            dma((2, 4)),
        ],
        compiler_params=pltpu.CompilerParams(
            collective_id=0, has_side_effects=True, vmem_limit_bytes=VMEM_LIMIT
        ),
        name="impact",
    )(
        displacement.reshape(whole), velocity.reshape(whole), modulus, density,
        clearance, mortar_coupling, owner, row, owner, row, offset, active,
    )
    shape = displacement.shape
    return new_disp.reshape(shape), new_vel.reshape(shape)


def solution(mesh):
    n_gx, n_gy = mesh.shape["gx"], mesh.shape["gy"]
    nodes = P(None, None, None, "gx", "gy")
    pairs = P("gx", "gy", None)
    return jax.shard_map(
        functools.partial(body, n_gx, n_gy),
        mesh=mesh,
        in_specs=(
            nodes, nodes, P(None, None, "gx", "gy"), P(None, None, "gx", "gy"), P("gx", "gy"), P(),
            pairs, pairs, pairs, pairs,
        ),
        out_specs=(nodes, nodes),
        check_vma=False,
    )
```

time: 82.3 us -> 69.7 us (0.85)
  Pallas kernels: 75.8 us -> 63.2 us
    pallas_call x1, Pallas kernels: 75.8 us -> 63.2 us  [body(): pl.pallas_call(functools.partial(kernel, n_gx, n_gy), out_shape=[jax.Shap...]
where the time goes in v2:
time: 69.7 us; the launch traced here: 69.6 us
  Pallas kernels  63.2 us (91%)
  local copies, waits for them, and re-layouts  5.73 us (8%)
    pallas_call x1, Pallas kernels, body(): pl.pallas_call(functools.partial(kernel, n_gx, n_gy), out_shape=[jax.Shap...  63.2 us
    unnamed x4, local copies, waits for them, and re-layouts  5.73 us

profile of v2, /device:TPU:1, one launch (start us, length us, event | category | flops | bytes accessed | tf_op | source)
XLA Modules:
  0.0 69.6 jit_solution(4954045847951648387)
XLA Ops:
  0.6 63.2 %impact.1 = (f32[6,8,128,128]{3,2,1,0:T(8,128)}, f32[6,8,128,128]{3,2,1,0:T(8,128)}) custom-call(f32[6,8,128,128]{3,2,1,0:T(8,128)} %bitcast.8, f32[6,8,128,128]{3,2,1,0:T(8,128)} %bitcast.9, f32[2,8,128,128]{3,2,1,0:T(8,128)} %mod.1, f32[2,8,128,128]{3,2,1,0:T(8,128)} %dens.1, f32[128,128]{1,0:T(8,128)} %clear.1, f32[128,128]{1,0:T(8,128)} %mortar.1, ...), custom_call_target="tpu_custom_call" | custom-call | tf_op jit(solution)/shard_map/impact/pallas_call | solution.py:487
  63.8 0.0 copy-start
  63.8 4.1 %copy.14 = f32[2,3,8,128,128]{4,3,2,1,0:T(8,128)} copy(f32[2,3,8,128,128]{4,3,2,1,0:T(8,128)} %bitcast.11) | data formatting | bytes 6291456
  67.9 0.0 copy-done
  67.9 1.7 %copy.15 = f32[2,3,8,128,128]{4,3,2,1,0:T(8,128)} copy(f32[2,3,8,128,128]{4,3,2,1,0:T(8,128)S(1)} %bitcast.10) | data formatting | bytes 6291456
Async XLA Ops:
  63.8 4.1 %copy-start = (f32[6,8,128,128]{3,2,1,0:T(8,128)S(1)}, f32[6,8,128,128]{3,2,1,0:T(8,128)}, u32[]{:S(2)}) copy-start(f32[6,8,128,128]{3,2,1,0:T(8,128)} %get-tuple-element.5) | copy-start | bytes 9437188

commit v3 on v2

--- a/solution.py
+++ b/solution.py
@@ -19,7 +19,7 @@
 time_step = 0.2
 penalty_stiffness = 4.0
 
-VMEM_LIMIT = 62 * 1024 * 1024
+VMEM_LIMIT = 54 * 1024 * 1024
 
 MESH = pl.DeviceIdType.MESH
 f32 = jnp.float32
@@ -40,10 +40,9 @@
 def kernel(
     n_gx, n_gy,
     disp, vel, mod, dens, clear, mortar, owner_s, row_s, owner_v, row_v, offset_v, active_v,
-    u_out, v_out,
     U, V, E, D, L, C, FACES, T, PART, RR, OH, FLAT, XS, YS, CS, HX, HY, HD, OFFS, ACT, SL, SF, ROWS, TR, DINV,
     load_sem, own_sem, halo_send, halo_recv, face_send, face_recv, pass_send, pass_recv,
-    core_send, core_recv, sum_send, sum_recv, store_sem,
+    core_send, core_recv, sum_send, sum_recv,
 ):
     gx = lax.axis_index("gx")
     gy = lax.axis_index("gy")
@@ -294,12 +293,12 @@
 
     def contact(step):
         def fetch(i, carry):
-            for k in range(8):
-                p = i * 8 + k
+            for k in range(32):
+                p = i * 32 + k
                 ROWS[pl.ds(p, 1), :] = FACES[step, pl.ds(owner_s[0, 0, p] * TILE + row_s[0, 0, p], 1), :]
             return carry
 
-        lax.fori_loop(0, PAIRS // 8, fetch, 0)
+        lax.fori_loop(0, PAIRS // 32, fetch, 0)
         offsets = OFFS[...]
         shifted = cyclic_shift(ROWS[...], offsets, -1)
         projected = shifted + jnp.dot(
@@ -329,15 +328,18 @@
     def first_sums(step, exchange):
         exchange.wait_recv()
         part = jnp.concatenate([split(PART[step, 0]), split(PART[step, 1])], axis=0)
-        targets = ((0, 1), (0, 3), (1, 0), (0, 1), (0, 3))
         out = []
         for k, there in enumerate(order):
             rows = rows_of(there)
             both = jnp.dot(OH[rows, :], part, preferred_element_type=f32)
             T[rows, :] = both[:, :TILE] + both[:, TILE:]
-            if k < len(targets):
-                out.append(send_sum(step, there, k, targets[k]))
+            if k < 3:
+                out.append(send_sum(step, there, k, ((0, 1), (0, 3), (1, 0))[k]))
         return out
+
+    def late_sums(step, out):
+        out.append(send_sum(step, (0, 1), 3, (0, 1)))
+        out.append(send_sum(step, (0, 3), 4, (0, 3)))
 
     def send_sum(step, there, k, target):
         copy = remote(
@@ -407,13 +409,15 @@
     loads[2].wait()
     DINV[...] = time_step / D[:, 0]
     half = BLOCKS * LAYERS // 2
-    couplings(0, half)
+    couplings(0, half // 2)
     finish_faces(0, copies, own)
     exchange = contact(0)
     for copy in halos:
         copy.wait_recv()
     spread(0, U, 0, 0, 3)
     out = first_sums(0, exchange)
+    couplings(half // 2, half)
+    late_sums(0, out)
     spread(0, U, 0, 3, 3)
     loads[3].wait()
     advance(0, BLOCKS)
@@ -426,10 +430,11 @@
     for copy in halos + stiff:
         copy.wait_send()
     halos = send_halos(1, U, 0, 0, 3)
-    advance(BLOCKS, 2 * BLOCKS)
+    advance(BLOCKS, BLOCKS + 14)
+    relay_faces(1, copies)
+    advance(BLOCKS + 14, 2 * BLOCKS)
     push(SLAVE, DINV[1] * SF[...])
     more = send_halos(2, U, 0, 3, 3)
-    relay_faces(1, copies)
     slave_gaps()
     for copy in out:
         copy.wait_send()
@@ -437,38 +442,25 @@
     for copy in halos:
         copy.wait_recv()
     spread(1, U, 0, 0, 3)
+    finish_faces(1, copies, own)
+    exchange = contact(1)
     for copy in more:
         copy.wait_recv()
     spread(2, U, 0, 3, 3)
-    finish_faces(1, copies, own)
-    exchange = contact(1)
+    out = first_sums(1, exchange)
     advance(0, 4)
-    out = first_sums(1, exchange)
-    advance(4, BLOCKS + 8)
+    late_sums(1, out)
+    advance(4, BLOCKS + 4)
     second_sums(1, out)
-    advance(BLOCKS + 8, 2 * BLOCKS)
+    advance(BLOCKS + 4, 2 * BLOCKS)
     push(SLAVE, DINV[1] * SF[...])
 
-    def store(k, block):
-        copies = [
-            pltpu.make_async_copy(ref.at[block], res.at[block], store_sem.at[which, k])
-            for which, (ref, res) in enumerate(((U, u_out), (V, v_out)))
-        ]
-        for copy in copies:
-            copy.start()
-        return copies
-
-    stores = store(0, (pl.ds(0, GROUPS), pl.ds(1, LAYERS - 1)))
-    stores += store(1, (pl.ds(0, 2), 0)) + store(2, (pl.ds(3, 3), 0))
     force = collect_forces(1, out)
     push(MASTER, -DINV[0] * force)
-    stores += store(3, (MASTER, 0))
     indices.wait_send()
     exchange.wait_send()
     for copy in out + halos + more:
         copy.wait_send()
-    for copy in stores:
-        copy.wait()
 
 
 def body(
@@ -486,12 +478,10 @@
     dma = pltpu.SemaphoreType.DMA
     new_disp, new_vel = pl.pallas_call(
         functools.partial(kernel, n_gx, n_gy),
-        out_shape=[jax.ShapeDtypeStruct(whole, f32)] * 2,
+        out_shape=[pltpu.VMEM(whole, f32)] * 2,
         in_specs=[hbm] * 4 + [vmem] * 2 + [smem] * 2 + [vmem] * 4,
-        out_specs=[hbm, hbm],
+        out_specs=[vmem, vmem],
         scratch_shapes=[
-            pltpu.VMEM(whole, f32),
-            pltpu.VMEM(whole, f32),
             pltpu.VMEM((2, LAYERS, TILE, TILE), f32),
             pltpu.VMEM((2, LAYERS, TILE, TILE), f32),
             pltpu.VMEM((3, 8, LAYERS, TILE + 16, TILE), f32),
@@ -522,7 +512,6 @@
             dma((STEPS, chips)), dma((STEPS, chips)),
             dma((3,)), dma((3,)),
             dma((STEPS, chips)), dma((STEPS, chips)),
-            dma((2, 4)),
         ],
         compiler_params=pltpu.CompilerParams(
             collective_id=0, has_side_effects=True, vmem_limit_bytes=VMEM_LIMIT

time: 69.7 us -> 64.7 us (0.928)
  Pallas kernels: 63.2 us -> 60.5 us
  local copies, waits for them, and re-layouts: 5.73 us -> 3.33 us
    pallas_call x1, Pallas kernels: 63.2 us -> 60.5 us  [body(): pl.pallas_call(functools.partial(kernel, n_gx, n_gy), out_shape=[pltpu.VM...]
    unnamed x4 -> x2, local copies, waits for them, and re-layouts: 5.73 us -> 3.33 us
where the time goes in v3:
time: 64.7 us; the launch traced here: 64.5 us
  Pallas kernels  60.5 us (94%)
  local copies, waits for them, and re-layouts  3.33 us (5%)
    pallas_call x1, Pallas kernels, body(): pl.pallas_call(functools.partial(kernel, n_gx, n_gy), out_shape=[pltpu.VM...  60.5 us
    unnamed x2, local copies, waits for them, and re-layouts  3.33 us

profile of v3, /device:TPU:1, one launch (start us, length us, event | category | flops | bytes accessed | tf_op | source)
XLA Modules:
  0.0 64.5 jit_solution(7307954079875438649)
XLA Ops:
  0.6 60.5 %impact.1 = (f32[6,8,128,128]{3,2,1,0:T(8,128)S(1)}, f32[6,8,128,128]{3,2,1,0:T(8,128)S(1)}) custom-call(f32[6,8,128,128]{3,2,1,0:T(8,128)} %bitcast.10, f32[6,8,128,128]{3,2,1,0:T(8,128)} %bitcast.11, f32[2,8,128,128]{3,2,1,0:T(8,128)} %mod.1, f32[2,8,128,128]{3,2,1,0:T(8,128)} %dens.1, f32[128,128]{1,0:T(8,128)} %clear.1, f32[128,128]{1,0:T(8,128)} %mortar.1, ...), custom_call_target="tpu_custom_call" | custom-call | tf_op jit(solution)/shard_map/impact/pallas_call | solution.py:479
  61.2 1.7 %copy.14 = f32[2,3,8,128,128]{4,3,2,1,0:T(8,128)} copy(f32[2,3,8,128,128]{4,3,2,1,0:T(8,128)S(1)} %bitcast.9) | data formatting | bytes 6291456
  62.9 1.7 %copy.15 = f32[2,3,8,128,128]{4,3,2,1,0:T(8,128)} copy(f32[2,3,8,128,128]{4,3,2,1,0:T(8,128)S(1)} %bitcast.8) | data formatting | bytes 6291456

commit v4 on v3

--- a/solution.py
+++ b/solution.py
@@ -394,8 +394,6 @@
             ).astype(jnp.bfloat16)
         return carry
 
-    lax.fori_loop(0, n_gy // 2, hot, 0)
-
     def slave_gaps():
         rest = clear[...] + U[SLAVE, 0]
         SL[pl.ds(0, TILE, stride=2), :] = rest
@@ -412,17 +410,17 @@
     couplings(0, half // 2)
     finish_faces(0, copies, own)
     exchange = contact(0)
-    for copy in halos:
-        copy.wait_recv()
-    spread(0, U, 0, 0, 3)
+    lax.fori_loop(0, n_gy // 2, hot, 0)
     out = first_sums(0, exchange)
     couplings(half // 2, half)
     late_sums(0, out)
-    spread(0, U, 0, 3, 3)
+    for copy in halos:
+        copy.wait_recv()
+    spread(0, U, 0, 0, GROUPS)
     loads[3].wait()
+    second_sums(0, out)
     advance(0, BLOCKS)
-    second_sums(0, out)
-    couplings(half, 2 * half)
+    couplings(half, half + half // 2)
     force = collect_forces(0, out)
     push(MASTER, -DINV[0] * force)
 
@@ -430,9 +428,10 @@
     for copy in halos + stiff:
         copy.wait_send()
     halos = send_halos(1, U, 0, 0, 3)
-    advance(BLOCKS, BLOCKS + 14)
+    couplings(half + half // 2, 2 * half)
+    advance(BLOCKS, BLOCKS + 8)
     relay_faces(1, copies)
-    advance(BLOCKS + 14, 2 * BLOCKS)
+    advance(BLOCKS + 8, 2 * BLOCKS)
     push(SLAVE, DINV[1] * SF[...])
     more = send_halos(2, U, 0, 3, 3)
     slave_gaps()
@@ -446,11 +445,11 @@
     exchange = contact(1)
     for copy in more:
         copy.wait_recv()
-    spread(2, U, 0, 3, 3)
+    spread(2, U, 0, 3, 1)
     out = first_sums(1, exchange)
-    advance(0, 4)
+    spread(2, U, 0, 4, 2)
     late_sums(1, out)
-    advance(4, BLOCKS + 4)
+    advance(0, BLOCKS + 4)
     second_sums(1, out)
     advance(BLOCKS + 4, 2 * BLOCKS)
     push(SLAVE, DINV[1] * SF[...])

time: 64.7 us -> 63.8 us (0.986)
  Pallas kernels: 60.5 us -> 59.6 us
    pallas_call x1, Pallas kernels: 60.5 us -> 59.6 us  [body(): pl.pallas_call(functools.partial(kernel, n_gx, n_gy), out_shape=[pltpu.VM...]
where the time goes in v4:
time: 63.8 us; the launch traced here: 63.6 us
  Pallas kernels  59.6 us (93%)
  local copies, waits for them, and re-layouts  3.33 us (5%)
  between operations  0.64 us (1%)
    pallas_call x1, Pallas kernels, body(): pl.pallas_call(functools.partial(kernel, n_gx, n_gy), out_shape=[pltpu.VM...  59.6 us
    unnamed x2, local copies, waits for them, and re-layouts  3.33 us

profile of v4, /device:TPU:1, one launch (start us, length us, event | category | flops | bytes accessed | tf_op | source)
XLA Modules:
  0.0 63.6 jit_solution(9143849730219056170)
XLA Ops:
  0.6 59.6 %impact.1 = (f32[6,8,128,128]{3,2,1,0:T(8,128)S(1)}, f32[6,8,128,128]{3,2,1,0:T(8,128)S(1)}) custom-call(f32[6,8,128,128]{3,2,1,0:T(8,128)} %bitcast.10, f32[6,8,128,128]{3,2,1,0:T(8,128)} %bitcast.11, f32[2,8,128,128]{3,2,1,0:T(8,128)} %mod.1, f32[2,8,128,128]{3,2,1,0:T(8,128)} %dens.1, f32[128,128]{1,0:T(8,128)} %clear.1, f32[128,128]{1,0:T(8,128)} %mortar.1, ...), custom_call_target="tpu_custom_call" | custom-call | tf_op jit(solution)/shard_map/impact/pallas_call | solution.py:478
  60.3 1.7 %copy.14 = f32[2,3,8,128,128]{4,3,2,1,0:T(8,128)} copy(f32[2,3,8,128,128]{4,3,2,1,0:T(8,128)S(1)} %bitcast.9) | data formatting | bytes 6291456
  61.9 1.7 %copy.15 = f32[2,3,8,128,128]{4,3,2,1,0:T(8,128)} copy(f32[2,3,8,128,128]{4,3,2,1,0:T(8,128)S(1)} %bitcast.8) | data formatting | bytes 6291456
